TPU v7x, 128 devices: a whole 4x4x4 slice. The times are simulated.
128 devices in a mesh: span: 16 (over y, z), wall: 8 (over x, core).
Axes of the slice: x: 4, y: 4, z: 4, core: 2. Of those that a mesh axis runs over, the one named last changes fastest.
Arguments:
- stress: float32 [2, 32, 1024, 2048], P(None, None, 'wall', 'span'), may hold values from -8 to 8
Outputs:
- pressure: float32 [2, 32, 1024, 2048], P(None, None, 'wall', 'span')
All inputs are finite; a program needn't handle non-finite values.
Results may differ from a plain program's by a relative error of at most 0.00035.
Values sent between devices are 32-bit elements; how exact they have to be, the bound alone decides.
A program may use at most 128 MiB of HBM per device.

v0:
```python
import math

import jax
import jax.numpy as jnp
from jax import lax
from jax.sharding import PartitionSpec as P

stretch_rate = 2.0
span_rate = 2.0 / 3.0
stream_rate = 0.25


def shifted(array, axis, by):
    peers = lax.axis_size(axis)
    pairs = [(i, i + by) for i in range(peers) if 0 <= i + by < peers]
    return lax.ppermute(array, axis, pairs)


def wall_coefficients(count):
    node_index = jnp.arange(count + 1, dtype=jnp.int32)
    xi_left = (2 * node_index - count - 1).astype(jnp.float32) / (count + 1)
    xi_right = (2 * node_index - count + 1).astype(jnp.float32) / (count + 1)
    spacing = jnp.sinh(2.0 * stretch_rate / (count + 1)) / (
        jnp.tanh(stretch_rate)
        * jnp.cosh(stretch_rate * xi_left)
        * jnp.cosh(stretch_rate * xi_right)
    )
    gap_before = spacing[:-1]
    gap_after = spacing[1:]
    lower_band = gap_after / (gap_before + gap_after)
    upper_band = gap_before / (gap_before + gap_after)
    weight = 0.5 * gap_before * gap_after
    return (lower_band, upper_band, weight)


def wave_squares(length, block_width, mode_ids):
    mode_index = jnp.arange(block_width, dtype=jnp.int32)
    signed = jnp.where(mode_index >= length // 2, mode_index - length, mode_index)
    span_wave = signed.astype(jnp.float32) * span_rate
    stream_wave = mode_ids.astype(jnp.float32) * stream_rate
    wave_sq = stream_wave[:, None] ** 2 + span_wave[None, :] ** 2
    return (wave_sq, span_wave**2)


def thomas(lower_band, upper_band, weight, wave_sq, rows):

    def forward(state, row_data):
        ratio_prev, value_prev = state
        low_entry, upp_entry, wei_entry, row_now = row_data
        pivot_value = 1.0 + wave_sq * wei_entry + low_entry * ratio_prev
        ratio_new = -upp_entry / pivot_value
        value_new = (row_now + low_entry * value_prev) / pivot_value
        return ((ratio_new, value_new), (ratio_new, value_new))

    start_state = (jnp.zeros(rows.shape[2:], jnp.float32), jnp.zeros(rows.shape[1:], jnp.float32))
    final_state, sweeps = lax.scan(
        forward, start_state, (lower_band, upper_band, weight, rows), unroll=4
    )

    def backward(after_value, row_data):
        ratio_now, value_now = row_data
        value_here = value_now - ratio_now[None] * after_value
        return (value_here, value_here)

    final_value, solution = lax.scan(
        backward, jnp.zeros(rows.shape[1:], jnp.float32), sweeps, reverse=True, unroll=4
    )
    return solution


def factor_pair(length):
    factor = 1
    for divisor in range(1, math.isqrt(length) + 1):
        if length % divisor == 0:
            factor = divisor
    return (factor, length // factor)


def phase_table(row_count, col_count, length, sign):
    row_ids = jnp.arange(row_count, dtype=jnp.int32)[:, None]
    col_ids = jnp.arange(col_count, dtype=jnp.int32)[None, :]
    angle_table = (row_ids * col_ids % length).astype(jnp.float32) * (2.0 * math.pi / length)
    return (jnp.cos(angle_table), sign * jnp.sin(angle_table))


def factored_dft(real_in, imag_in, sign):
    length = real_in.shape[-1]
    inner_len, outer_len = factor_pair(length)
    leading = real_in.shape[:-1]
    real_grid = real_in.reshape(leading + (outer_len, inner_len))
    imag_grid = imag_in.reshape(leading + (outer_len, inner_len))
    cos_outer, sin_outer = phase_table(outer_len, outer_len, outer_len, sign)
    high = lax.Precision.HIGHEST
    first_real = jnp.einsum("...za,zm->...ma", real_grid, cos_outer, precision=high) - jnp.einsum(
        "...za,zm->...ma", imag_grid, sin_outer, precision=high
    )
    first_imag = jnp.einsum("...za,zm->...ma", real_grid, sin_outer, precision=high) + jnp.einsum(
        "...za,zm->...ma", imag_grid, cos_outer, precision=high
    )
    cos_twid, sin_twid = phase_table(outer_len, inner_len, length, sign)
    twid_real = first_real * cos_twid - first_imag * sin_twid
    twid_imag = first_real * sin_twid + first_imag * cos_twid
    cos_inner, sin_inner = phase_table(inner_len, inner_len, inner_len, sign)
    last_real = jnp.einsum("...ma,an->...nm", twid_real, cos_inner, precision=high) - jnp.einsum(
        "...ma,an->...nm", twid_imag, sin_inner, precision=high
    )
    last_imag = jnp.einsum("...ma,an->...nm", twid_real, sin_inner, precision=high) + jnp.einsum(
        "...ma,an->...nm", twid_imag, cos_inner, precision=high
    )
    return (last_real.reshape(leading + (length,)), last_imag.reshape(leading + (length,)))


def body(stress):
    mode_count = stress.shape[1]
    rows_dev = stress.shape[2]
    span_count = lax.axis_size("span")
    wall_count = lax.axis_size("wall")
    mode_dev = mode_count // span_count
    length = stress.shape[3] * span_count
    wall_cells = rows_dev * wall_count
    wall_at = lax.axis_index("wall")
    span_at = lax.axis_index("span")
    lower_all, upper_all, weight_all = wall_coefficients(wall_cells)
    row_start = wall_at * rows_dev
    lower_band = lax.dynamic_slice_in_dim(lower_all, row_start, rows_dev)
    upper_band = lax.dynamic_slice_in_dim(upper_all, row_start, rows_dev)
    weight = lax.dynamic_slice_in_dim(weight_all, row_start, rows_dev)
    mode_ids = span_at * mode_dev + jnp.arange(mode_dev, dtype=jnp.int32)
    wave_sq, span_sq = wave_squares(length, length, mode_ids)
    received = lax.all_to_all(stress, "span", split_axis=1, concat_axis=3, tiled=True)
    real_part, imag_part = factored_dft(received[0], received[1], -1.0)
    stacked = jnp.stack([real_part, imag_part], axis=0)
    spectral = jnp.transpose(stacked, (2, 0, 1, 3))
    source = spectral * weight[:, None, None, None] * span_sq[None, None, None, :]
    inner = rows_dev - 1
    row_index = jnp.arange(inner, dtype=jnp.int32)
    alpha_col = jnp.where(row_index == 0, lower_band[0], 0.0)
    beta_col = jnp.where(row_index == inner - 1, upper_band[inner - 1], 0.0)
    upper_inner = jnp.where(row_index == inner - 1, 0.0, upper_band[:inner])
    ones_block = jnp.ones((inner, 1, mode_dev, length), jnp.float32)
    extended = jnp.concatenate(
        [
            source[:inner],
            ones_block * alpha_col[:, None, None, None],
            ones_block * beta_col[:, None, None, None],
        ],
        axis=1,
    )
    local_part = thomas(lower_band[:inner], upper_inner, weight[:inner], wave_sq, extended)
    next_rows = shifted(local_part[0], "wall", -1)
    last_rows = local_part[inner - 1]
    sep_lower = lower_band[inner]
    sep_upper = upper_band[inner]
    sep_diag = 1.0 + wave_sq * weight[inner]
    coef_a = -sep_lower * last_rows[2]
    coef_b = sep_diag - sep_lower * last_rows[3] - sep_upper * next_rows[2]
    coef_c = -sep_upper * next_rows[3]
    coef_r = source[inner] + sep_lower * last_rows[0:2] + sep_upper * next_rows[0:2]
    levels = wall_count.bit_length() - 1
    for level in range(levels):
        stride = 1 << level
        packed = jnp.concatenate([coef_a[None], coef_b[None], coef_c[None], coef_r], axis=0)
        below_rows = shifted(packed, "wall", stride)
        above_rows = shifted(packed, "wall", -stride)
        below_pivot = below_rows[1] + (wall_at < stride).astype(jnp.float32)
        above_pivot = above_rows[1] + (wall_at + stride >= wall_count).astype(jnp.float32)
        left_factor = coef_a / below_pivot
        right_factor = coef_c / above_pivot
        new_a = -left_factor * below_rows[0]
        new_c = -right_factor * above_rows[2]
        new_b = coef_b - left_factor * below_rows[2] - right_factor * above_rows[0]
        new_r = coef_r - left_factor[None] * below_rows[3:5] - right_factor[None] * above_rows[3:5]
        coef_a, coef_b, coef_c, coef_r = (new_a, new_b, new_c, new_r)
    value_here = coef_r / coef_b[None]
    value_prev = shifted(value_here, "wall", 1)
    inner_rows = (
        local_part[:, 0:2]
        + local_part[:, 2:3] * value_prev[None]
        + local_part[:, 3:4] * value_here[None]
    )
    pressure_rows = jnp.concatenate([inner_rows, value_here[None]], axis=0)
    back_real, back_imag = factored_dft(pressure_rows[:, 0], pressure_rows[:, 1], 1.0)
    stacked = jnp.stack([back_real / length, back_imag / length], axis=0)
    physical = jnp.transpose(stacked, (0, 2, 1, 3))
    return lax.all_to_all(physical, "span", split_axis=3, concat_axis=1, tiled=True)


def solution(mesh):
    placed = (P(None, None, "wall", "span"),)
    return jax.shard_map(
        body, mesh=mesh, in_specs=placed, out_specs=P(None, None, "wall", "span"), check_vma=False
    )
```

profile of v0, /device:TPU:1, one launch (start us, length us, event | category | flops | bytes accessed | tf_op | source)
XLA Modules:
  0.0 899.3 jit_solution(15733420314305276271)
XLA Ops:
  4.7 8.6 all-to-all-start
  20.8 54.0 %all-to-all-done = f32[2,32,128,128]{3,2,0,1:T(8,128)} async-done(((f32[2,32,128,128]{3,2,0,1:T(8,128)}), f32[2,32,128,128]{3,2,0,1:T(8,128)}, u32[]{:S(2)}, u32[]{:S(2)}) %all-to-all-start) | async-done | bytes 4194336 | tf_op jit(solution)/shard_map/all_to_all | solution.py:130
  119.6 13.7 %slice_reduce_fusion.2 = (f32[4,2,2048]{2,1,0:T(2,128)S(1)}, f32[4,2,2048]{2,1,0:T(2,128)S(1)}, f32[4,2,2048]{2,1,0:T(2,128)S(1)}) fusion(f32[127,4,2,2048]{0,3,2,1:T(8,128)S(1)} %pad_maximum_fusion), kind=kLoop, calls=%fused_computation.57 | loop fusion | bytes 393216 | tf_op jit(solution)/shard_map/slice | solution.py:56
  133.2 13.4 %copy.210 = f32[124,4,2,2048]{3,2,1,0:T(2,128)} copy(f32[124,4,2,2048]{0,3,2,1:T(8,128)} %bitcast.361) | data formatting | bytes 16252928 | tf_op jit(solution)/shard_map/slice | solution.py:56
  146.6 7.3 broadcast.408.clone
  153.9 447.0 %while.34 = (s32[]{:T(128)}, f32[2,2048]{1,0:T(2,128)S(1)}, f32[4,2,2048]{2,1,0:T(2,128)S(1)}, f32[31,4,2,2048]{3,2,1,0:T(2,128)}, f32[31,4,4,2,2048]{4,3,2,1,0:...) while((s32[]{:T(128)}, f32[2,2048]{1,0:T(2,128)S(1)}, ...), condition=%wide.region_1.2_spmd.clone, body=%wide.region_0.1_spmd.clone.sunk | while | flops 548874 | bytes 1466900 | solution.py:56
  158.3 4.9 broadcast_divide_fusion.12
  187.2 4.9 broadcast_divide_fusion.12
  201.6 4.9 broadcast_divide_fusion.12
  216.0 4.9 broadcast_divide_fusion.12
  230.4 4.9 broadcast_divide_fusion.12
  244.8 4.9 broadcast_divide_fusion.12
  259.2 4.9 broadcast_divide_fusion.12
  273.6 4.9 broadcast_divide_fusion.12
  609.7 8.3 pad_maximum_fusion.2
  618.1 7.3 broadcast.408
  625.4 86.7 %while.35 = (s32[]{:T(128)}, f32[4,2,2048]{2,1,0:T(2,128)S(1)}, f32[31,4,4,2,2048]{4,3,2,1,0:T(2,128)}, f32[31,4,4,2,2048]{4,3,2,1,0:T(2,128)}, f32[31,4,2,2048]...) while((s32[]{:T(128)}, f32[4,2,2048]{2,1,0:T(2,128)S(1)}, ...), condition=%wide.region_3.4_spmd.clone, body=%wide.region_2.3_spmd.clone.sunk | while | flops 376839 | bytes 1458395 | solution.py:65
  722.4 6.3 fusion.27
  751.3 5.5 collective-permute-start.5
  756.9 7.9 pad_maximum_fusion.1
  771.9 6.4 fusion.30
  821.2 10.5 %copy.227 = f32[2,2,128,2048]{2,1,0,3:T(2,128)S(1)} copy(f32[2,2,128,2048]{2,3,1,0:T(8,128)S(1)} %maximum_bitcast_fusion.3) | data formatting | bytes 8388608 | tf_op jit(solution)/shard_map/transpose | solution.py:184
  831.7 59.8 %all_to_all.33 = f32[2,2,128,2048]{2,1,0,3:T(2,128)S(1)} all-to-all(f32[2,2,128,2048]{2,1,0,3:T(2,128)S(1)} %copy.227), channel_id=1, replica_groups=mesh['span'=16,'wall'=8] {'span'}, dimensions={3} | all-to-all | bytes 8388608 | tf_op jit(solution)/shard_map/all_to_all | solution.py:185
  893.7 5.3 copy.229
  (505 shorter events, 564.5 us)
Async XLA Ops:
  4.7 70.2 %all-to-all-start = ((f32[2,32,128,128]{3,2,0,1:T(8,128)}), f32[2,32,128,128]{3,2,0,1:T(8,128)}, u32[]{:S(2)}, u32[]{:S(2)}) async-start(f32[2,32,128,128]{3,2,0,1:T(8,128)} %copy.196), calls=%async_computation | async-start | bytes 8388608 | tf_op jit(solution)/shard_map/all_to_all | solution.py:130
  92.6 4.9 copy-start.2
  117.0 2.0 copy-start.1
  119.6 13.7 %copy-start = (f32[127,4,2,2048]{0,3,2,1:T(8,128)}, f32[127,4,2,2048]{0,3,2,1:T(8,128)S(1)}, u32[]{:S(2)}) copy-start(f32[127,4,2,2048]{0,3,2,1:T(8,128)S(1)} %pad_maximum_fusion) | copy-start | bytes 24969220
  715.5 13.3 %collective-permute-start = (f32[4,2,2048]{2,1,0:T(2,128)S(1)}, f32[4,2,2048]{2,1,0:T(2,128)S(1)}, u32[]{:S(2)}, u32[]{:S(2)}) collective-permute-start(f32[4,2,2048]{2,1,0:T(2,128)S(1)} %fusion.86), channel_id=1, source_target_pairs={{1,0},{2,1},{3,2},{4,3},{5,4},{6,5},{7,6},{9,8},{10,9},{11,10},{12... | collective-permute-start | bytes 196616 | tf_op jit(solution)/shard_map/ppermute | solution.py:16
  732.1 5.0 collective-permute-start.1
  735.1 5.8 collective-permute-start.2
  741.0 4.7 collective-permute-start.3
  744.2 5.7 collective-permute-start.4
  750.0 14.7 %collective-permute-start.6 = (f32[5,2,2048]{2,1,0:T(2,128)S(1)}, f32[5,2,2048]{2,1,0:T(2,128)S(1)}, u32[]{:S(2)}, u32[]{:S(2)}) collective-permute-start(f32[5,2,2048]{2,1,0:T(2,128)S(1)} %pad_maximum_fusion.11), channel_id=1, source_target_pairs={{4,0},{5,1},{6,2},{7,3},{12,8},{13,9},{14,10},{15,11},{20,16},{21,... | collective-permute-start | bytes 245768 | tf_op jit(solution)/shard_map/ppermute | solution.py:16
  751.3 13.4 %collective-permute-start.5 = (f32[5,2,2048]{2,1,0:T(2,128)S(1)}, f32[5,2,2048]{2,1,0:T(2,128)S(1)}, u32[]{:S(2)}, u32[]{:S(2)}) collective-permute-start(f32[5,2,2048]{2,1,0:T(2,128)S(1)} %pad_maximum_fusion.11), channel_id=1, source_target_pairs={{0,4},{1,5},{2,6},{3,7},{8,12},{9,13},{10,14},{11,15},{16,20},{17,... | collective-permute-start | bytes 245768 | tf_op jit(solution)/shard_map/ppermute | solution.py:16
  756.8 12.1 %slice-start = ((s8[8126464]{0:T(1024)(128)(4,1)}), s8[4194304]{0:T(1024)(128)(4,1)S(1)}, s32[]{:S(2)}) async-start(s8[8126464]{0:T(1024)(128)(4,1)} %bitcast.367), calls=%async_computation.2 | async-start | bytes 8388608
  756.9 12.1 %slice-start.1 = ((s8[8126464]{0:T(1024)(128)(4,1)}), s8[3932160]{0:T(1024)(128)(4,1)S(1)}, s32[]{:S(2)}) async-start(s8[8126464]{0:T(1024)(128)(4,1)} %bitcast.367), calls=%async_computation.3 | async-start | bytes 7864320
  764.8 7.1 collective-permute-start.7
  796.8 4.9 copy-start.3
where the time goes:
time: 916 us; the launch traced here: 899 us
  other arithmetic  449 us (49%)
  local copies, waits for them, and re-layouts  154 us (17%)
  loops' own time  77 us (8%)
  waiting for transfers between devices  61.4 us (7%)
  matrix products  60.8 us (7%)
  blocking collectives  59.8 us (7%)
  starting transfers between devices  33.2 us (4%)
    div x31, other arithmetic, forward(): ratio_new = -upp_entry / pivot_value  153 us
    div x31, other arithmetic, forward(): value_new = (row_now + low_entry * value_prev) / pivot_value  109 us
    slice x96, local copies, waits for them, and re-layouts, thomas(): lax.scan(forward, start_state, (lower_band, upper_band, weight, rows), un...  88.1 us
    another operation x1, loops' own time, thomas(): lax.scan(forward, start_state, (lower_band, upper_band, weight, rows), un...  76.8 us
    dynamic_update_slice x93, other arithmetic, thomas(): lax.scan(forward, start_state, (lower_band, upper_band, weight, rows), un...  72.8 us
    all_to_all x1, blocking collectives, body(): lax.all_to_all(physical, 'span', split_axis=3, concat_axis=1, tiled=True)  59.8 us
    all_to_all x1, waiting for transfers between devices, body(): lax.all_to_all(stress, 'span', split_axis=1, concat_axis=3, tiled=True)  54 us
    broadcast_in_dim x32, other arithmetic, thomas(): lax.scan(backward, jnp.zeros(rows.shape[1:], jnp.float32), sweeps, revers...  32.1 us
  transfers between devices with their start and end apart: 9, of which 4 were waited for; matrix products, arithmetic and copies ran while one was open for 3% of the time, Pallas kernels for 0%

commit v1 on v0

v1 whole, which is shorter than its diff:
```python
import math

import jax
import jax.numpy as jnp
import ml_dtypes
import numpy as np
from jax import lax
from jax.experimental import pallas as pl
from jax.experimental.pallas import tpu as pltpu
from jax.sharding import PartitionSpec as P

MESH = pl.DeviceIdType.MESH
F32 = jnp.float32
BF16 = jnp.bfloat16

NZ, NY, KX = 2048, 1024, 32
SPAN, WALL = 16, 8
ROWS = NY // WALL
CELLS = NZ // SPAN
MODES = KX // SPAN
LAST = ROWS - 1
STRETCH = 2.0
UNROLL = 8

OFFSETS = [(2, 2), (1, 1), (3, 3), (0, 2), (1, 3), (3, 1), (2, 0), (2, 1), (1, 2), (2, 3), (3, 2),
           (0, 1), (1, 0), (0, 3), (3, 0)]


def tables():
    index = np.arange(CELLS)
    angle = 2.0 * math.pi * (np.outer(index, index) % CELLS) / CELLS
    cos, sin = np.cos(angle), np.sin(angle)
    there = np.block([[cos, -sin], [sin, cos]])
    back = np.block([[cos, sin], [-sin, cos]]) / NZ
    mats = []
    for full in (there, back):
        high = full.astype(np.float32).astype(ml_dtypes.bfloat16)
        mats += [high, (full - high.astype(np.float64)).astype(ml_dtypes.bfloat16)]
    twist = 2.0 * math.pi * np.outer(np.arange(SPAN), index) / NZ
    return np.stack(mats), np.stack([np.cos(twist), np.sin(twist)]).astype(np.float32)


def times(value, cos, sin):
    re, im = value
    return re * cos - im * sin, re * sin + im * cos


def four(x, sign):
    (ar, ai), (br, bi), (cr, ci), (dr, di) = x
    er, ei, fr, fi = ar + cr, ai + ci, ar - cr, ai - ci
    gr, gi, hr, hi = br + dr, bi + di, br - dr, bi - di
    if sign > 0:
        return [(er + gr, ei + gi), (fr - hi, fi + hr), (er - gr, ei - gi), (fr + hi, fi - hr)]
    return [(er + gr, ei + gi), (fr + hi, fi - hr), (er - gr, ei - gi), (fr - hi, fi + hr)]


def sixteen(x, sign):
    half = math.sqrt(0.5)
    first = [four([x[4 * i + j] for i in range(4)], sign) for j in range(4)]
    out = [None] * 16
    for k in range(4):
        col = []
        for j in range(4):
            re, im = first[j][k]
            power = j * k
            if power == 0:
                col.append((re, im))
            elif power == 2:
                col.append(((re - sign * im) * half, (im + sign * re) * half))
            elif power == 4:
                col.append((-im, re) if sign > 0 else (im, -re))
            elif power == 6:
                col.append(((-re - sign * im) * half, (sign * re - im) * half))
            else:
                angle = 2.0 * math.pi * power / 16
                col.append(times((re, im), math.cos(angle), sign * math.sin(angle)))
        for p, value in enumerate(four(col, sign)):
            out[k + 4 * p] = value
    return out


def product(x, high, low):
    x_high = x.astype(BF16)
    x_low = (x - x_high.astype(F32)).astype(BF16)
    dot = lambda a, b: jnp.dot(a, b, preferred_element_type=F32)
    return dot(x_high, high) + (dot(x_low, high) + dot(x_high, low))


def kernel(x_ref, mats_hbm, twist_hbm, o_ref, land, stage, grid, spec, vals, low_s, upp_s, wei_s,
           t_gain, t_carry, t_ratio, t_above, t_below, lhs, sep, rhs, solved, seps, mats, twist,
           there_s, there_r, back_s, back_r, wall_s, wall_r, local):
    me = lax.axis_index("span")
    wall = lax.axis_index("wall")
    y, z = me // 4, me % 4

    def peer(offset):
        return lax.rem(y + offset[0], 4) * 4 + lax.rem(z + offset[1], 4)

    barrier = pltpu.get_barrier_semaphore()
    for offset in OFFSETS:
        pl.semaphore_signal(barrier, inc=1, device_id={"span": peer(offset)}, device_id_type=MESH)
    for k in range(1, WALL):
        pl.semaphore_signal(barrier, inc=1, device_id={"wall": lax.rem(wall + k, WALL)}, device_id_type=MESH)
    pl.semaphore_wait(barrier, SPAN - 1 + WALL - 1)

    there, back = {}, {}
    for mode in range(MODES):
        for j, offset in enumerate(OFFSETS):
            to = peer(offset)
            there[mode, j] = pltpu.make_async_remote_copy(
                src_ref=x_ref.at[:, MODES * to + mode], dst_ref=land.at[mode, me],
                send_sem=there_s.at[mode, j], recv_sem=there_r.at[mode, j],
                device_id={"span": to}, device_id_type=MESH)
            back[mode, j] = pltpu.make_async_remote_copy(
                src_ref=stage.at[mode, to], dst_ref=o_ref.at[:, MODES * me + mode],
                send_sem=back_s.at[mode, j], recv_sem=back_r.at[mode, j],
                device_id={"span": to}, device_id_type=MESH)
    for mode in range(MODES):
        for j in range(len(OFFSETS)):
            there[mode, j].start()
    own = [pltpu.make_async_copy(x_ref.at[:, MODES * me + mode], land.at[mode, me], local.at[mode])
           for mode in range(MODES)]
    consts = [pltpu.make_async_copy(mats_hbm, mats, local.at[2]), pltpu.make_async_copy(twist_hbm, twist, local.at[3])]
    for copy in own + consts:
        copy.start()

    scale = math.sinh(2.0 * STRETCH / (NY + 1)) / math.tanh(STRETCH)

    def bands(cell):
        def cosh(k):
            xi = (2 * (cell + k) - (NY + 1)).astype(F32) * F32(STRETCH / (NY + 1))
            return 0.5 * (jnp.exp(xi) + jnp.exp(-xi))
        c0, c1, c2 = cosh(0), cosh(1), cosh(2)
        total = c0 + c2
        return c0 / total, c2 / total, (0.5 * scale * scale) / (c0 * c2 * (c1 * c1))

    cell = lax.broadcasted_iota(jnp.int32, (ROWS, 128), 0) + wall * ROWS
    low, upp, wei = bands(cell)
    low_s[...] = low
    upp_s[...] = upp
    wei_s[...] = wei
    sep_cell = lax.broadcasted_iota(jnp.int32, (WALL, 128), 0) * ROWS + LAST
    _, sep_upp, _ = bands(sep_cell)
    seps[...] = sep_upp

    freq = lax.broadcasted_iota(jnp.int32, (SPAN, CELLS), 1) * SPAN + lax.broadcasted_iota(jnp.int32, (SPAN, CELLS), 0)
    freq = jnp.where(freq >= NZ // 2, freq - NZ, freq)
    span_sq = jnp.square(freq.astype(F32) * F32(2.0 / 3.0))
    wave = [span_sq + jnp.square((me * MODES + mode).astype(F32) * F32(0.25)) for mode in range(MODES)]
    one = jnp.ones((SPAN, CELLS), F32)
    zero = jnp.zeros((SPAN, CELLS), F32)

    def at(row):
        return pl.ds(pl.multiple_of(row * SPAN, SPAN), SPAN)

    def row_of(ref, row):
        return jnp.broadcast_to(ref[pl.ds(row, 1), :], (SPAN, CELLS))

    def down(row, tops):
        low, upp, wei = row_of(low_s, row), row_of(upp_s, row), row_of(wei_s, row)
        new = []
        for mode in range(MODES):
            d = wave[mode] * wei + low * tops[mode]
            inv = 1.0 / (d + upp)
            t_gain[mode, at(row), :] = span_sq * (wei * inv)
            t_carry[mode, at(row), :] = low * inv
            t_ratio[mode, at(row), :] = upp * inv
            new.append(d * inv)
        return tuple(new)

    tops = lax.fori_loop(0, LAST, down, (one,) * MODES)
    low_l, wei_l = row_of(low_s, LAST), row_of(wei_s, LAST)
    for mode in range(MODES):
        lhs[wall, mode, 0] = wave[mode] * wei_l + low_l * tops[mode]
        t_gain[mode, at(LAST), :] = zero
        t_carry[mode, at(LAST), :] = zero
        t_ratio[mode, at(LAST), :] = zero
        t_above[mode, at(LAST), :] = zero
        t_below[mode, at(LAST), :] = one

    def up(i, state):
        row = LAST - 1 - i
        low, upp, wei = row_of(low_s, row), row_of(upp_s, row), row_of(wei_s, row)
        new = []
        for mode in range(MODES):
            under, below = state[mode]
            e = wave[mode] * wei + upp * under
            inv = 1.0 / (e + low)
            t_above[mode, at(row), :] = low * inv
            below = below * t_ratio[mode, at(row), :]
            t_below[mode, at(row), :] = below
            new.append((e * inv, below))
        return tuple(new)

    ends = lax.fori_loop(0, LAST, up, ((one, one),) * MODES)

    def across(row, state):
        new = []
        for mode in range(MODES):
            above = state[mode] * t_above[mode, at(row), :]
            t_above[mode, at(row), :] = above
            new.append(above)
        return tuple(new)

    above = lax.fori_loop(0, LAST, across, (one,) * MODES)
    for mode in range(MODES):
        lhs[wall, mode, 1] = low_l * above[mode]
        lhs[wall, mode, 2] = ends[mode][0]
        lhs[wall, mode, 3] = ends[mode][1]

    def to_wall(ref, group):
        copies = []
        for k in range(1, WALL):
            copy = pltpu.make_async_remote_copy(
                src_ref=ref, dst_ref=ref, send_sem=wall_s.at[group, k], recv_sem=wall_r.at[group, k],
                device_id={"wall": lax.rem(wall + k, WALL)}, device_id_type=MESH)
            copy.start()
            copies.append(copy)
        return copies

    lhs_copies = to_wall(lhs.at[wall], MODES)
    for copy in lhs_copies:
        copy.wait_recv()
    for mode in range(MODES):
        ratio = zero
        for w in range(WALL):
            sep_up = row_of(seps, w)
            last = w == WALL - 1
            pivot = lhs[w, mode, 0] + (sep_up if last else sep_up * lhs[w + 1, mode, 2])
            link = lhs[w, mode, 1]
            inv = 1.0 / (pivot - link * ratio if w else pivot)
            ratio = zero if last else sep_up * lhs[w + 1, mode, 3] * inv
            sep[mode, w, 0] = inv
            sep[mode, w, 1] = link * inv if w else zero
            sep[mode, w, 2] = ratio

    for copy in own + consts:
        copy.wait()
    own = []
    wall_copies = []
    for mode in range(MODES):
        for j in range(len(OFFSETS)):
            there[mode, j].wait_recv()

        def outer(i, carry):
            rows = pl.ds(pl.multiple_of(i * 8, 8), 8)
            block = [(land[mode, s, 0, rows, :], land[mode, s, 1, rows, :]) for s in range(SPAN)]
            for b, (re, im) in enumerate(sixteen(block, -1)):
                cos = jnp.broadcast_to(twist[0, b:b + 1, :], (8, CELLS))
                sin = jnp.broadcast_to(twist[1, b:b + 1, :], (8, CELLS))
                into = pl.ds(pl.multiple_of(b * ROWS + i * 8, 8), 8)
                grid[0, into, :] = re * cos + im * sin
                grid[1, into, :] = im * cos - re * sin
            return carry

        lax.fori_loop(0, ROWS // 8, outer, 0)

        def inner(i, carry):
            rows = pl.ds(pl.multiple_of(i * 512, 512), 512)
            both = product(jnp.concatenate([grid[0, rows, :], grid[1, rows, :]], axis=1), mats[0], mats[1])
            spec[0, rows, :] = both[:, :CELLS]
            spec[1, rows, :] = both[:, CELLS:]
            return carry

        lax.fori_loop(0, NZ // 512, inner, 0)

        def forward(i, state):
            prev = list(state)
            for k in range(UNROLL):
                row = i * UNROLL + k
                gain, carry = t_gain[mode, at(row), :], t_carry[mode, at(row), :]
                for c in range(2):
                    prev[c] = spec[c, pl.ds(row, SPAN, stride=ROWS), :] * gain + carry * prev[c]
                    vals[c, at(row), :] = prev[c]
            return tuple(prev)

        lax.fori_loop(0, ROWS // UNROLL, forward, (zero, zero))

        def backward(i, state):
            after = list(state)
            for k in range(UNROLL):
                row = LAST - (i * UNROLL + k)
                ratio = t_ratio[mode, at(row), :]
                for c in range(2):
                    after[c] = vals[c, at(row), :] + ratio * after[c]
                    vals[c, at(row), :] = after[c]
            return tuple(after)

        final = [vals[c, at(LAST - 1), :] for c in range(2)]
        first = lax.fori_loop(0, ROWS // UNROLL, backward, (zero, zero))
        for c in range(2):
            source = spec[c, pl.ds(LAST, SPAN, stride=ROWS), :] * (span_sq * wei_l)
            rhs[mode, wall, 0, c] = source + low_l * final[c]
            rhs[mode, wall, 1, c] = first[c]
        copies = to_wall(rhs.at[mode, wall], mode)
        wall_copies += copies
        for copy in copies:
            copy.wait_recv()

        for c in range(2):
            value, values = None, []
            for w in range(WALL):
                r = rhs[mode, w, 0, c]
                if w < WALL - 1:
                    r = r + row_of(seps, w) * rhs[mode, w + 1, 1, c]
                value = r * sep[mode, w, 0] if w == 0 else r * sep[mode, w, 0] + sep[mode, w, 1] * value
                values.append(value)
            for w in range(WALL - 2, -1, -1):
                values[w] = values[w] + sep[mode, w, 2] * values[w + 1]
            for w in range(WALL):
                solved[w, c] = values[w]
        here = [solved[wall, c] for c in range(2)]
        up_at = lax.rem(wall + WALL - 1, WALL)
        there_is = (wall > 0).astype(F32)
        over = [solved[up_at, c] * there_is for c in range(2)]

        def inner_back(i, carry):
            rows = pl.ds(pl.multiple_of(i * 512, 512), 512)
            shape = (512 // SPAN, SPAN, CELLS)
            above = t_above[mode, rows, :].reshape(shape)
            below = t_below[mode, rows, :].reshape(shape)
            parts = [
                (vals[c, rows, :].reshape(shape) + above * over[c][None] + below * here[c][None]).reshape(512, CELLS)
                for c in range(2)]
            both = product(jnp.concatenate(parts, axis=1), mats[2], mats[3])
            re, im = both[:, :CELLS].reshape(shape), both[:, CELLS:].reshape(shape)
            cos, sin = twist[0][None], twist[1][None]
            grid[0, rows, :] = (re * cos - im * sin).reshape(512, CELLS)
            grid[1, rows, :] = (re * sin + im * cos).reshape(512, CELLS)
            return carry

        lax.fori_loop(0, NZ // 512, inner_back, 0)

        def outer_back(i, carry):
            block = [(grid[0, pl.ds(i * (8 * SPAN) + b, 8, stride=SPAN), :],
                      grid[1, pl.ds(i * (8 * SPAN) + b, 8, stride=SPAN), :]) for b in range(SPAN)]
            rows = pl.ds(pl.multiple_of(i * 8, 8), 8)
            for s, (re, im) in enumerate(sixteen(block, 1)):
                stage[mode, s, 0, rows, :] = re
                stage[mode, s, 1, rows, :] = im
            return carry

        lax.fori_loop(0, ROWS // 8, outer_back, 0)

        if mode == 0:
            for m in range(MODES):
                for j in range(len(OFFSETS)):
                    there[m, j].wait_send()
        for j in range(len(OFFSETS)):
            back[mode, j].start()
        copy = pltpu.make_async_copy(stage.at[mode, me], o_ref.at[:, MODES * me + mode], local.at[mode])
        copy.start()
        own.append(copy)

    for copy in lhs_copies + wall_copies:
        copy.wait_send()
    for mode in range(MODES):
        own[mode].wait()
        for j in range(len(OFFSETS)):
            back[mode, j].wait()


def solution(mesh):
    mats, twist = tables()

    def body(stress):
        vmem = lambda *shape: pltpu.VMEM(shape, F32)
        dma = lambda *shape: pltpu.SemaphoreType.DMA(shape)
        table = (MODES, NZ * ROWS // CELLS, CELLS)
        return pl.pallas_call(
            kernel,
            out_shape=jax.ShapeDtypeStruct(stress.shape, F32),
            in_specs=[pl.BlockSpec(memory_space=pltpu.HBM)] * 3,
            out_specs=pl.BlockSpec(memory_space=pltpu.VMEM),
            scratch_shapes=[
                vmem(MODES, SPAN, 2, ROWS, CELLS),
                vmem(MODES, SPAN, 2, ROWS, CELLS),
                vmem(2, SPAN * ROWS, CELLS),
                vmem(2, SPAN * ROWS, CELLS),
                vmem(2, SPAN * ROWS, CELLS),
                vmem(ROWS, 128), vmem(ROWS, 128), vmem(ROWS, 128),
                vmem(*table), vmem(*table), vmem(*table), vmem(*table), vmem(*table),
                vmem(WALL, MODES, 4, SPAN, CELLS),
                vmem(MODES, WALL, 3, SPAN, CELLS),
                vmem(MODES, WALL, 2, 2, SPAN, CELLS),
                vmem(WALL, 2, SPAN, CELLS),
                vmem(WALL, 128),
                pltpu.VMEM((4, 2 * CELLS, 2 * CELLS), BF16),
                vmem(2, SPAN, CELLS),
                dma(MODES, SPAN), dma(MODES, SPAN), dma(MODES, SPAN), dma(MODES, SPAN),
                dma(MODES + 1, WALL), dma(MODES + 1, WALL), dma(4),
            ],
            name="pressure",
            compiler_params=pltpu.CompilerParams(
                collective_id=1, has_side_effects=True, vmem_limit_bytes=56 << 20),
        )(stress, mats, twist)

    placed = P(None, None, "wall", "span")
    return jax.shard_map(body, mesh=mesh, in_specs=(placed,), out_specs=placed, check_vma=False)
```

time: 916 us -> 116 us (0.13)
  the two profiles are of different devices: /device:TPU:1 before, /device:TPU:105 now
where the time goes in v1:
time: 116 us
  Pallas kernels  111 us (96%)
  local copies, waits for them, and re-layouts  4.7 us (4%)
    pallas_call x1, Pallas kernels, body(): pl.pallas_call(kernel, out_shape=jax.ShapeDtypeStruct(stress.shape, F32),...  111 us
    unnamed x1, local copies, waits for them, and re-layouts  4.7 us

profile of v1, /device:TPU:105, one launch (start us, length us, event | category | flops | bytes accessed | tf_op | source)
XLA Modules:
  0.0 115.6 jit_solution(7043171057812332267)
XLA Ops:
  0.0 110.9 %pressure.1 = f32[2,32,128,128]{3,2,1,0:T(8,128)} custom-call(f32[2,32,128,128]{3,2,1,0:T(8,128)} %x_ref.1, bf16[4,256,256]{2,1,0:T(8,128)(2,1)} %constant.4.clone.mats_hbm, f32[2,16,128]{2,1,0:T(8,128)} %constant.5.clone.twist_hbm), custom_call_target="tpu_custom_call" | custom-call | tf_op jit(solution)/shard_map/pressure/pallas_call | solution.py:370
  110.9 4.7 %copy.5 = f32[2,32,128,128]{3,2,1,0:T(8,128)} copy(f32[2,32,128,128]{3,2,1,0:T(8,128)} %pressure.1) | data formatting | bytes 8388608

commit v2 on v1

--- a/solution.py
+++ b/solution.py
@@ -2,8 +2,6 @@
 
 import jax
 import jax.numpy as jnp
-import ml_dtypes
-import numpy as np
 from jax import lax
 from jax.experimental import pallas as pl
 from jax.experimental.pallas import tpu as pltpu
@@ -24,20 +22,7 @@
 
 OFFSETS = [(2, 2), (1, 1), (3, 3), (0, 2), (1, 3), (3, 1), (2, 0), (2, 1), (1, 2), (2, 3), (3, 2),
            (0, 1), (1, 0), (0, 3), (3, 0)]
-
-
-def tables():
-    index = np.arange(CELLS)
-    angle = 2.0 * math.pi * (np.outer(index, index) % CELLS) / CELLS
-    cos, sin = np.cos(angle), np.sin(angle)
-    there = np.block([[cos, -sin], [sin, cos]])
-    back = np.block([[cos, sin], [-sin, cos]]) / NZ
-    mats = []
-    for full in (there, back):
-        high = full.astype(np.float32).astype(ml_dtypes.bfloat16)
-        mats += [high, (full - high.astype(np.float64)).astype(ml_dtypes.bfloat16)]
-    twist = 2.0 * math.pi * np.outer(np.arange(SPAN), index) / NZ
-    return np.stack(mats), np.stack([np.cos(twist), np.sin(twist)]).astype(np.float32)
+PIECES = [(offset, part) for part in range(2) for offset in OFFSETS]
 
 
 def times(value, cos, sin):
@@ -86,7 +71,7 @@
     return dot(x_high, high) + (dot(x_low, high) + dot(x_high, low))
 
 
-def kernel(x_ref, mats_hbm, twist_hbm, o_ref, land, stage, grid, spec, vals, low_s, upp_s, wei_s,
+def kernel(x_ref, o_ref, land, stage, grid, spec, vals, low_s, upp_s, wei_s,
            t_gain, t_carry, t_ratio, t_above, t_below, lhs, sep, rhs, solved, seps, mats, twist,
            there_s, there_r, back_s, back_r, wall_s, wall_r, local):
     me = lax.axis_index("span")
@@ -105,24 +90,38 @@
 
     there, back = {}, {}
     for mode in range(MODES):
-        for j, offset in enumerate(OFFSETS):
+        for j, (offset, part) in enumerate(PIECES):
             to = peer(offset)
             there[mode, j] = pltpu.make_async_remote_copy(
-                src_ref=x_ref.at[:, MODES * to + mode], dst_ref=land.at[mode, me],
+                src_ref=x_ref.at[part, MODES * to + mode], dst_ref=land.at[mode, me, part],
                 send_sem=there_s.at[mode, j], recv_sem=there_r.at[mode, j],
                 device_id={"span": to}, device_id_type=MESH)
             back[mode, j] = pltpu.make_async_remote_copy(
-                src_ref=stage.at[mode, to], dst_ref=o_ref.at[:, MODES * me + mode],
+                src_ref=stage.at[mode, to, part], dst_ref=o_ref.at[part, MODES * me + mode],
                 send_sem=back_s.at[mode, j], recv_sem=back_r.at[mode, j],
                 device_id={"span": to}, device_id_type=MESH)
     for mode in range(MODES):
-        for j in range(len(OFFSETS)):
+        for j in range(len(PIECES)):
             there[mode, j].start()
     own = [pltpu.make_async_copy(x_ref.at[:, MODES * me + mode], land.at[mode, me], local.at[mode])
            for mode in range(MODES)]
-    consts = [pltpu.make_async_copy(mats_hbm, mats, local.at[2]), pltpu.make_async_copy(twist_hbm, twist, local.at[3])]
-    for copy in own + consts:
+    for copy in own:
         copy.start()
+
+    def circle(rows, length):
+        shape = (rows, CELLS)
+        steps = lax.broadcasted_iota(jnp.int32, shape, 0) * lax.broadcasted_iota(jnp.int32, shape, 1)
+        angle = lax.rem(steps, length).astype(F32) * F32(2.0 * math.pi / length)
+        return jnp.cos(angle), jnp.sin(angle)
+
+    twist[0], twist[1] = circle(SPAN, NZ)
+    cos, sin = circle(CELLS, CELLS)
+    for which, (re, im) in enumerate([(cos, -sin), (cos * F32(1 / NZ), sin * F32(1 / NZ))]):
+        for r, c, value in [(0, 0, re), (0, 1, im), (1, 0, -im), (1, 1, re)]:
+            high = value.astype(BF16)
+            place = (pl.ds(r * CELLS, CELLS), pl.ds(c * CELLS, CELLS))
+            mats[2 * which, *place] = high
+            mats[2 * which + 1, *place] = (value - high.astype(F32)).astype(BF16)
 
     scale = math.sinh(2.0 * STRETCH / (NY + 1)) / math.tanh(STRETCH)
 
@@ -234,12 +233,12 @@
             sep[mode, w, 1] = link * inv if w else zero
             sep[mode, w, 2] = ratio
 
-    for copy in own + consts:
+    for copy in own:
         copy.wait()
     own = []
     wall_copies = []
     for mode in range(MODES):
-        for j in range(len(OFFSETS)):
+        for j in range(len(PIECES)):
             there[mode, j].wait_recv()
 
         def outer(i, carry):
@@ -344,9 +343,9 @@
 
         if mode == 0:
             for m in range(MODES):
-                for j in range(len(OFFSETS)):
+                for j in range(len(PIECES)):
                     there[m, j].wait_send()
-        for j in range(len(OFFSETS)):
+        for j in range(len(PIECES)):
             back[mode, j].start()
         copy = pltpu.make_async_copy(stage.at[mode, me], o_ref.at[:, MODES * me + mode], local.at[mode])
         copy.start()
@@ -356,13 +355,11 @@
         copy.wait_send()
     for mode in range(MODES):
         own[mode].wait()
-        for j in range(len(OFFSETS)):
+        for j in range(len(PIECES)):
             back[mode, j].wait()
 
 
 def solution(mesh):
-    mats, twist = tables()
-
     def body(stress):
         vmem = lambda *shape: pltpu.VMEM(shape, F32)
         dma = lambda *shape: pltpu.SemaphoreType.DMA(shape)
@@ -370,8 +367,8 @@
         return pl.pallas_call(
             kernel,
             out_shape=jax.ShapeDtypeStruct(stress.shape, F32),
-            in_specs=[pl.BlockSpec(memory_space=pltpu.HBM)] * 3,
-            out_specs=pl.BlockSpec(memory_space=pltpu.VMEM),
+            in_specs=[pl.BlockSpec(memory_space=pltpu.HBM)],
+            out_specs=pl.BlockSpec(memory_space=pl.ANY),
             scratch_shapes=[
                 vmem(MODES, SPAN, 2, ROWS, CELLS),
                 vmem(MODES, SPAN, 2, ROWS, CELLS),
@@ -387,13 +384,13 @@
                 vmem(WALL, 128),
                 pltpu.VMEM((4, 2 * CELLS, 2 * CELLS), BF16),
                 vmem(2, SPAN, CELLS),
-                dma(MODES, SPAN), dma(MODES, SPAN), dma(MODES, SPAN), dma(MODES, SPAN),
-                dma(MODES + 1, WALL), dma(MODES + 1, WALL), dma(4),
+                dma(MODES, len(PIECES)), dma(MODES, len(PIECES)), dma(MODES, len(PIECES)), dma(MODES, len(PIECES)),
+                dma(MODES + 1, WALL), dma(MODES + 1, WALL), dma(MODES),
             ],
             name="pressure",
             compiler_params=pltpu.CompilerParams(
-                collective_id=1, has_side_effects=True, vmem_limit_bytes=56 << 20),
-        )(stress, mats, twist)
+                collective_id=1, has_side_effects=True, vmem_limit_bytes=48 << 20),
+        )(stress)
 
     placed = P(None, None, "wall", "span")
     return jax.shard_map(body, mesh=mesh, in_specs=(placed,), out_specs=placed, check_vma=False)

time: 116 us -> 105 us (0.905)
  the two profiles are of different devices: /device:TPU:105 before, /device:TPU:1 now
where the time goes in v2:
time: 105 us
  Pallas kernels  103 us (98%)
  local copies, waits for them, and re-layouts  2.02 us (2%)
    pallas_call x1, Pallas kernels, body(): pl.pallas_call(kernel, out_shape=jax.ShapeDtypeStruct(stress.shape, F32),...  103 us

profile of v2, /device:TPU:1, one launch (start us, length us, event | category | flops | bytes accessed | tf_op | source)
XLA Modules:
  0.0 105.0 jit_solution(3330245687688618859)
XLA Ops:
  0.0 102.9 %pressure.1 = f32[2,32,128,128]{3,2,1,0:T(8,128)S(1)} custom-call(f32[2,32,128,128]{3,2,1,0:T(8,128)} %x_ref.1), custom_call_target="tpu_custom_call" | custom-call | tf_op jit(solution)/shard_map/pressure/pallas_call | solution.py:367
  102.9 2.0 %copy.3 = f32[2,32,128,128]{3,2,1,0:T(8,128)} copy(f32[2,32,128,128]{3,2,1,0:T(8,128)S(1)} %pressure.1) | data formatting | bytes 8388608

commit v3 on v2

--- a/solution.py
+++ b/solution.py
@@ -23,6 +23,8 @@
 OFFSETS = [(2, 2), (1, 1), (3, 3), (0, 2), (1, 3), (3, 1), (2, 0), (2, 1), (1, 2), (2, 3), (3, 2),
            (0, 1), (1, 0), (0, 3), (3, 0)]
 PIECES = [(offset, part) for part in range(2) for offset in OFFSETS]
+EARLY = [(0, j) for j in range(30)] + [(1, j) for j in range(15)]
+GATES = (EARLY, [(1, j) for j in range(15, 30)])
 
 
 def times(value, cos, sin):
@@ -100,9 +102,8 @@
                 src_ref=stage.at[mode, to, part], dst_ref=o_ref.at[part, MODES * me + mode],
                 send_sem=back_s.at[mode, j], recv_sem=back_r.at[mode, j],
                 device_id={"span": to}, device_id_type=MESH)
-    for mode in range(MODES):
-        for j in range(len(PIECES)):
-            there[mode, j].start()
+    for j in range(len(PIECES)):
+        there[0, j].start()
     own = [pltpu.make_async_copy(x_ref.at[:, MODES * me + mode], land.at[mode, me], local.at[mode])
            for mode in range(MODES)]
     for copy in own:
@@ -218,20 +219,24 @@
         return copies
 
     lhs_copies = to_wall(lhs.at[wall], MODES)
-    for copy in lhs_copies:
-        copy.wait_recv()
-    for mode in range(MODES):
-        ratio = zero
-        for w in range(WALL):
-            sep_up = row_of(seps, w)
-            last = w == WALL - 1
-            pivot = lhs[w, mode, 0] + (sep_up if last else sep_up * lhs[w + 1, mode, 2])
-            link = lhs[w, mode, 1]
-            inv = 1.0 / (pivot - link * ratio if w else pivot)
-            ratio = zero if last else sep_up * lhs[w + 1, mode, 3] * inv
-            sep[mode, w, 0] = inv
-            sep[mode, w, 1] = link * inv if w else zero
-            sep[mode, w, 2] = ratio
+    for j in range(len(PIECES)):
+        there[1, j].start()
+
+    def factor():
+        for copy in lhs_copies:
+            copy.wait_recv()
+        for mode in range(MODES):
+            ratio = zero
+            for w in range(WALL):
+                sep_up = row_of(seps, w)
+                last = w == WALL - 1
+                pivot = lhs[w, mode, 0] + (sep_up if last else sep_up * lhs[w + 1, mode, 2])
+                link = lhs[w, mode, 1]
+                inv = 1.0 / (pivot - link * ratio if w else pivot)
+                ratio = zero if last else sep_up * lhs[w + 1, mode, 3] * inv
+                sep[mode, w, 0] = inv
+                sep[mode, w, 1] = link * inv if w else zero
+                sep[mode, w, 2] = ratio
 
     for copy in own:
         copy.wait()
@@ -293,6 +298,8 @@
             rhs[mode, wall, 1, c] = first[c]
         copies = to_wall(rhs.at[mode, wall], mode)
         wall_copies += copies
+        if mode == 0:
+            factor()
         for copy in copies:
             copy.wait_recv()
 
@@ -341,10 +348,8 @@
 
         lax.fori_loop(0, ROWS // 8, outer_back, 0)
 
-        if mode == 0:
-            for m in range(MODES):
-                for j in range(len(PIECES)):
-                    there[m, j].wait_send()
+        for m, j in GATES[mode]:
+            there[m, j].wait_send()
         for j in range(len(PIECES)):
             back[mode, j].start()
         copy = pltpu.make_async_copy(stage.at[mode, me], o_ref.at[:, MODES * me + mode], local.at[mode])

time: 105 us -> 105 us (level)
  no operation moved by 1% of the time
where the time goes in v3:
time: 105 us; the launch traced here: 104 us
  Pallas kernels  102 us (97%)
  local copies, waits for them, and re-layouts  2.02 us (2%)
    pallas_call x1, Pallas kernels, body(): pl.pallas_call(kernel, out_shape=jax.ShapeDtypeStruct(stress.shape, F32),...  102 us

profile of v3, /device:TPU:1, one launch (start us, length us, event | category | flops | bytes accessed | tf_op | source)
XLA Modules:
  0.0 103.9 jit_solution(9702762438325184352)
XLA Ops:
  0.0 101.9 %pressure.1 = f32[2,32,128,128]{3,2,1,0:T(8,128)S(1)} custom-call(f32[2,32,128,128]{3,2,1,0:T(8,128)} %x_ref.1), custom_call_target="tpu_custom_call" | custom-call | tf_op jit(solution)/shard_map/pressure/pallas_call | solution.py:372
  101.9 2.0 %copy.3 = f32[2,32,128,128]{3,2,1,0:T(8,128)} copy(f32[2,32,128,128]{3,2,1,0:T(8,128)S(1)} %pressure.1) | data formatting | bytes 8388608

commit v4 on v3

--- a/solution.py
+++ b/solution.py
@@ -21,9 +21,10 @@
 UNROLL = 8
 
 OFFSETS = [(2, 2), (1, 1), (3, 3), (0, 2), (1, 3), (3, 1), (2, 0), (2, 1), (1, 2), (2, 3), (3, 2),
-           (0, 1), (1, 0), (0, 3), (3, 0)]
+           (1, 0), (0, 1), (3, 0), (0, 3)]
 PIECES = [(offset, part) for part in range(2) for offset in OFFSETS]
 EARLY = [(0, j) for j in range(30)] + [(1, j) for j in range(15)]
+HELD = 15
 GATES = (EARLY, [(1, j) for j in range(15, 30)])
 
 
@@ -300,6 +301,9 @@
         wall_copies += copies
         if mode == 0:
             factor()
+        else:
+            for j in range(HELD, len(PIECES)):
+                back[0, j].start()
         for copy in copies:
             copy.wait_recv()
 
@@ -350,7 +354,7 @@
 
         for m, j in GATES[mode]:
             there[m, j].wait_send()
-        for j in range(len(PIECES)):
+        for j in range(HELD if mode == 0 else len(PIECES)):
             back[mode, j].start()
         copy = pltpu.make_async_copy(stage.at[mode, me], o_ref.at[:, MODES * me + mode], local.at[mode])
         copy.start()

time: 105 us -> 105 us (level)
  no operation moved by 1% of the time
where the time goes in v4:
time: 105 us; the launch traced here: 104 us
  Pallas kernels  102 us (97%)
  local copies, waits for them, and re-layouts  2.02 us (2%)
    pallas_call x1, Pallas kernels, body(): pl.pallas_call(kernel, out_shape=jax.ShapeDtypeStruct(stress.shape, F32),...  102 us

profile of v4, /device:TPU:1, one launch (start us, length us, event | category | flops | bytes accessed | tf_op | source)
XLA Modules:
  0.0 103.9 jit_solution(8545182009812431479)
XLA Ops:
  0.0 101.8 %pressure.1 = f32[2,32,128,128]{3,2,1,0:T(8,128)S(1)} custom-call(f32[2,32,128,128]{3,2,1,0:T(8,128)} %x_ref.1), custom_call_target="tpu_custom_call" | custom-call | tf_op jit(solution)/shard_map/pressure/pallas_call | solution.py:376
  101.8 2.0 %copy.3 = f32[2,32,128,128]{3,2,1,0:T(8,128)} copy(f32[2,32,128,128]{3,2,1,0:T(8,128)S(1)} %pressure.1) | data formatting | bytes 8388608

commit v5 on v4

--- a/solution.py
+++ b/solution.py
@@ -24,7 +24,7 @@
            (1, 0), (0, 1), (3, 0), (0, 3)]
 PIECES = [(offset, part) for part in range(2) for offset in OFFSETS]
 EARLY = [(0, j) for j in range(30)] + [(1, j) for j in range(15)]
-HELD = 15
+HELD = 10
 GATES = (EARLY, [(1, j) for j in range(15, 30)])
 
 

time: 105 us -> 106 us (level)
  no operation moved by 1% of the time
where the time goes in v5:
time: 106 us; the launch traced here: 105 us
  Pallas kernels  103 us (97%)
  local copies, waits for them, and re-layouts  2.02 us (2%)
    pallas_call x1, Pallas kernels, body(): pl.pallas_call(kernel, out_shape=jax.ShapeDtypeStruct(stress.shape, F32),...  103 us

profile of v5, /device:TPU:1, one launch (start us, length us, event | category | flops | bytes accessed | tf_op | source)
XLA Modules:
  0.0 104.7 jit_solution(1982650910836204203)
XLA Ops:
  0.0 102.7 %pressure.1 = f32[2,32,128,128]{3,2,1,0:T(8,128)S(1)} custom-call(f32[2,32,128,128]{3,2,1,0:T(8,128)} %x_ref.1), custom_call_target="tpu_custom_call" | custom-call | tf_op jit(solution)/shard_map/pressure/pallas_call | solution.py:376
  102.7 2.0 %copy.3 = f32[2,32,128,128]{3,2,1,0:T(8,128)} copy(f32[2,32,128,128]{3,2,1,0:T(8,128)S(1)} %pressure.1) | data formatting | bytes 8388608
